TPU v7x, 32 devices: a whole 2x2x4 slice. The times are simulated.
32 devices in a mesh: groups: 2 (over x), dp: 8 (over z, y), tensor: 2 (over core).
Axes of the slice: x: 2, y: 2, z: 4, core: 2. Of those that a mesh axis runs over, the one named last changes fastest.
Arguments:
- hidden_states: bfloat16 [3584, 5120], P(('groups', 'dp'), 'tensor'), parts along dimension 0, may hold values from -6 to 6
- input_gain: float32 [5120], replicated, may hold values from 0.1 to 1.9
- q_weight: bfloat16 [5120, 512], P(None, 'tensor'), may hold values from -0.078125 to 0.078125
- k_weight: bfloat16 [5120, 256], P(None, 'tensor'), may hold values from -0.078125 to 0.078125
- v_weight: bfloat16 [5120, 256], P(None, 'tensor'), may hold values from -0.078125 to 0.078125
- o_weight: bfloat16 [512, 5120], P('tensor'), may hold values from -0.25 to 0.25
- q_gain: float32 [128], replicated, may hold values from 0.6 to 13
- k_gain: float32 [128], replicated, may hold values from 0.6 to 13
- seq_lens: int32 [16, 5], P('groups'), parts along dimension 0, may hold values from 1 to 160, as said below
- dest: int32 [16, 5], P('groups'), parts along dimension 0, may hold values from 0 to 7, as said below
Outputs:
- mixed: bfloat16 [2560, 5120], P(('groups', 'dp'), 'tensor'), parts along dimension 0
There are 2 independent parts, one for each index of `groups`. A program takes and returns all parts, laid end to end along the dimension named above; an argument that names none is the same for every part. Nothing has to cross between parts.
Inputs may be any that keep to these rules, and one draw needn't show every extreme that they name: `seq_lens`: each replica's sequences lie packed from row 0 of its block in slot order. `dest`: slot 0 never moves. A replica either sends sequences or receives them, never both. At most 16 tokens in all go from one replica to any one other, and at most 160 tokens are processed by one replica; both bounds are reached.
All inputs are finite; a program needn't handle non-finite values.
Results may differ from a plain program's by a relative error of at most 0.004.
The roundings to bfloat16 on the way count: a program that leaves them out, or rounds other values in their place, can miss the bound.
Values may be sent and summed in bfloat16 or wider, within the bound.
A program may use at most 128 MiB of HBM per device.

v0:
```python
import jax
import jax.numpy as jnp
from jax import lax
from jax.sharding import PartitionSpec as P

HD = 128
CAPP = 16
LONG = 160
SHORT = 8


EPSILON = 1e-06
ROPE_BASE = 1000000.0
MASKED_SCORE = -1e30


def rms_scale(entries, gain):
    mean_square = jnp.mean(entries * entries, axis=-1, keepdims=True)
    return entries * lax.rsqrt(mean_square + EPSILON) * gain


def rotation(positions, width):
    half_head = width // 2
    frequency = ROPE_BASE ** (-2.0 * jnp.arange(half_head, dtype=jnp.float32) / width)
    angles = positions.astype(jnp.float32)[:, None] * frequency[None, :]
    return (jnp.cos(angles), jnp.sin(angles))


def rotate(entries, cosine, sine_part):
    half_head = entries.shape[-1] // 2
    first_half = entries[..., :half_head]
    second_half = entries[..., half_head:]
    return jnp.concatenate(
        [
            first_half * cosine - second_half * sine_part,
            second_half * cosine + first_half * sine_part,
        ],
        axis=-1,
    )


def sequence_table(seq_lens, dest):
    replicas, slots = seq_lens.shape
    lengths = seq_lens.reshape(-1)
    offsets = (jnp.cumsum(seq_lens, axis=1) - seq_lens).reshape(-1)
    source = jnp.broadcast_to(
        jnp.arange(replicas, dtype=jnp.int32)[:, None], (replicas, slots)
    ).reshape(-1)
    slot_index = jnp.broadcast_to(
        jnp.arange(slots, dtype=jnp.int32)[None, :], (replicas, slots)
    ).reshape(-1)
    target = dest.reshape(-1)
    order_key = (source - target) % replicas * slots + slot_index
    earlier = (target[None, :] == target[:, None]) & (order_key[None, :] < order_key[:, None])
    begins = jnp.sum(jnp.where(earlier, lengths[None, :], 0), axis=1)
    return (source, slot_index, lengths, target, offsets, begins)


def widen(half_rows):
    return lax.all_gather(half_rows, "tensor", axis=1, tiled=True)


def project(full_rows, positions, input_gain, q_weight, k_weight, v_weight, q_gain, k_gain):
    row_count = full_rows.shape[0]
    normed = rms_scale(full_rows.astype(jnp.float32), input_gain).astype(jnp.bfloat16)
    cosine, sine_part = rotation(positions, HD)
    queries = jnp.dot(normed, q_weight, preferred_element_type=jnp.float32).reshape(
        row_count, -1, HD
    )
    queries = rotate(rms_scale(queries, q_gain), cosine[:, None, :], sine_part[:, None, :]).astype(
        jnp.bfloat16
    )
    key_rows = jnp.dot(normed, k_weight, preferred_element_type=jnp.float32)
    key_rows = rotate(rms_scale(key_rows, k_gain), cosine, sine_part).astype(jnp.bfloat16)
    value_rows = jnp.dot(normed, v_weight, preferred_element_type=jnp.float32).astype(jnp.bfloat16)
    return (queries, key_rows, value_rows)


def attend(queries, key_rows, value_rows, segment, position):
    scores = jnp.einsum(
        "qhd,kd->hqk", queries, key_rows, preferred_element_type=jnp.float32
    ) * queries.shape[-1] ** (-0.5)
    allowed = (segment[:, None] == segment[None, :]) & (position[None, :] <= position[:, None])
    scores = jnp.where(allowed[None], scores, MASKED_SCORE)
    row_max = jnp.max(scores, axis=2, keepdims=True)
    exp_scores = jnp.exp(scores - row_max)
    weights = (exp_scores / jnp.sum(exp_scores, axis=2, keepdims=True)).astype(jnp.bfloat16)
    return jnp.einsum("hqk,kd->qhd", weights, value_rows, preferred_element_type=jnp.float32)


def per_device(
    hidden_states,
    input_gain,
    q_weight,
    k_weight,
    v_weight,
    o_weight,
    q_gain,
    k_gain,
    seq_lens,
    dest,
):
    replicas = lax.axis_size("dp")
    replica = lax.axis_index("dp")
    tensor_part = lax.axis_index("tensor")
    home_rows, half_width = hidden_states.shape
    slots = seq_lens.shape[1]
    work_rows = max(LONG, slots * SHORT + (slots - 1) * CAPP)
    source, slot_index, lengths, target, offsets, begins = sequence_table(seq_lens, dest)
    seq_ident = jnp.arange(lengths.shape[0], dtype=jnp.int32)
    shipped_seq = source != target
    pair_earlier = (
        (source[None, :] == source[:, None])
        & (target[None, :] == target[:, None])
        & (slot_index[None, :] < slot_index[:, None])
    )
    send_begin = jnp.sum(jnp.where(pair_earlier, lengths[None, :], 0), axis=1)
    peer_ids = jnp.arange(replicas, dtype=jnp.int32)[:, None, None]
    slot_rows = jnp.arange(CAPP, dtype=jnp.int32)[None, :, None]
    inside = (send_begin <= slot_rows) & (slot_rows < send_begin + lengths)
    outgoing = inside & shipped_seq & (source == replica) & (target == peer_ids)
    send_rows = jnp.sum(jnp.where(outgoing, offsets + slot_rows - send_begin, 0), axis=2).reshape(
        -1
    )
    incoming = inside & shipped_seq & (target == replica) & (source == peer_ids)
    arrive_live = jnp.any(incoming, axis=2)
    arrive_seg = jnp.where(arrive_live, jnp.sum(jnp.where(incoming, seq_ident, 0), axis=2), -1)
    arrive_pos = jnp.sum(jnp.where(incoming, slot_rows - send_begin, 0), axis=2)
    home_ids = jnp.arange(home_rows, dtype=jnp.int32)[:, None]
    resident = (source == replica) & (offsets <= home_ids) & (home_ids < offsets + lengths)
    home_live = jnp.any(resident, axis=1)
    home_seg = jnp.where(home_live, jnp.sum(jnp.where(resident, seq_ident, 0), axis=1), -1)
    home_pos = jnp.sum(jnp.where(resident, home_ids - offsets, 0), axis=1)
    work_ids = jnp.arange(work_rows, dtype=jnp.int32)[:, None]
    placed = (target == replica) & (begins <= work_ids) & (work_ids < begins + lengths)
    work_live = jnp.any(placed, axis=1)
    work_pos = jnp.sum(jnp.where(placed, work_ids - begins, 0), axis=1)
    pool_base = jnp.where(source == replica, offsets, home_rows + source * CAPP + send_begin)
    pool_row = jnp.sum(jnp.where(placed, pool_base, 0), axis=1) + work_pos
    home_full = widen(hidden_states)
    outbound = jnp.take(home_full, send_rows, axis=0).reshape(replicas, CAPP, -1)
    arrived = lax.all_to_all(outbound, "dp", split_axis=0, concat_axis=0, tiled=True)
    pool_full = jnp.concatenate([home_full, arrived.reshape(replicas * CAPP, -1)], axis=0)
    pool_half = lax.dynamic_slice_in_dim(pool_full, tensor_part * half_width, half_width, 1)
    pool_pos = jnp.concatenate([home_pos, arrive_pos.reshape(-1)], axis=0)
    queries, key_rows, value_rows = project(
        pool_full, pool_pos, input_gain, q_weight, k_weight, v_weight, q_gain, k_gain
    )
    home_out = attend(
        queries[:home_rows], key_rows[:home_rows], value_rows[:home_rows], home_seg, home_pos
    )
    arrive_out = jax.vmap(attend)(
        queries[home_rows:].reshape(replicas, CAPP, -1, HD),
        key_rows[home_rows:].reshape(replicas, CAPP, HD),
        value_rows[home_rows:].reshape(replicas, CAPP, HD),
        arrive_seg,
        arrive_pos,
    )
    head_out = jnp.concatenate([home_out, arrive_out.reshape(replicas * CAPP, -1, HD)], axis=0)
    head_out = head_out.reshape(home_rows + replicas * CAPP, -1).astype(jnp.bfloat16)
    all_heads = lax.all_gather(head_out, "tensor", axis=1, tiled=True)
    own_columns = lax.all_to_all(o_weight, "tensor", split_axis=1, concat_axis=0, tiled=True)
    summed = jnp.dot(all_heads, own_columns, preferred_element_type=jnp.float32)
    mixed_pool = pool_half.astype(jnp.float32) + summed
    mixed = jnp.where(work_live[:, None], jnp.take(mixed_pool, pool_row, axis=0), 0.0)
    return mixed.astype(jnp.bfloat16)


def solution(mesh):
    return jax.shard_map(
        per_device,
        mesh=mesh,
        in_specs=(
            P(("groups", "dp"), "tensor"),
            P(),
            P(None, "tensor"),
            P(None, "tensor"),
            P(None, "tensor"),
            P("tensor", None),
            P(),
            P(),
            P("groups", None),
            P("groups", None),
        ),
        out_specs=P(("groups", "dp"), "tensor"),
        check_vma=False,
    )
```

profile of v0, /device:TPU:0, one launch (start us, length us, event | category | flops | bytes accessed | tf_op | source)
XLA Modules:
  0.0 107.7 jit_solution(4255287312289752939)
XLA Ops:
  6.5 0.7 all-gather.2.cloned.1.call-update
  7.3 4.5 %copy.54 = bf16[256,5120]{0,1:T(8,128)(2,1)} copy(bf16[256,5120]{1,0:T(8,128)(2,1)} %param.15) | data formatting | bytes 5242880 | tf_op args[5]
  11.7 5.1 %all-to-all-start.1 = ((bf16[256,2,2560]{0,2,1:T(8,128)(2,1)}), bf16[256,2,2560]{0,2,1:T(8,128)(2,1)}, u32[]{:S(2)}, u32[]{:S(2)}) async-start(bf16[256,2,2560]{0,2,1:T(8,128)(2,1)} %bitcast.82), calls=%async_computation.1 | async-start | bytes 5242880 | tf_op jit(solution)/shard_map/all_to_all | solution.py:162
  17.5 0.2 select_reduce_fusion.6
  17.7 0.2 select_reduce_fusion
  18.1 4.4 %all-gather.2.cloned.1.call-done = bf16[224,5120]{1,0:T(8,128)(2,1)} async-done(((bf16[224,2560]{1,0:T(8,128)(2,1)}), bf16[224,5120]{1,0:T(8,128)(2,1)}) %all-gather.2.cloned.1.call-update) | async-done | bytes 2293776 | tf_op jit(solution)/shard_map/all_gather | solution.py:60
  22.5 5.6 %gather_fusion = bf16[128,5120]{1,0:T(8,128)(2,1)} fusion(bf16[224,5120]{1,0:T(8,128)(2,1)} %all-gather.2.cloned.1.call-done, s32[1024]{0:T(1024)S(1)} %pad_clamp_fusion.1), kind=kCustom, calls=%fused_computation | custom fusion | bytes 2621952 | tf_op jit(solution)/shard_map/jit(_take)/gather | solution.py:141
  28.1 2.6 %broadcast_select_fusion = bf16[8,16,5120]{2,1,0:T(8,128)(2,1)} fusion(bf16[8,16,5120]{2,1,0:T(8,128)(2,1)} %bitcast.83, pred[8,16]{1,0:T(8,128)(4,1)S(1)} %compare_and_fusion.4), kind=kLoop, calls=%fused_computation.15 | loop fusion | flops 655360 | bytes 2621568 | tf_op jit(solution)/shard_map/jit(_take)/select_n | solution.py:141
  30.7 6.5 %all-to-all-start = ((bf16[8,16,5120]{2,1,0:T(8,128)(2,1)}), bf16[8,16,5120]{2,1,0:T(8,128)(2,1)}, u32[]{:S(2)}, u32[]{:S(2)}) async-start(bf16[8,16,5120]{2,1,0:T(8,128)(2,1)} %broadcast_select_fusion), calls=%async_computation | async-start | bytes 2621440 | tf_op jit(solution)/shard_map/all_to_all | solution.py:142
  37.2 0.3 fusion.20
  37.6 4.4 %copy.55 = bf16[2,256,2560]{2,1,0:T(8,128)(2,1)} copy(bf16[2,256,2560]{1,2,0:T(8,128)(2,1)} %bitcast.17) | data formatting | bytes 5242880 | tf_op jit(solution)/shard_map/all_to_all | solution.py:162
  42.0 0.5 multiply_power_fusion
  42.9 0.2 and_reduce_fusion
  43.5 0.8 compare_and_fusion
  44.2 24.8 %all-to-all-done = bf16[8,16,5120]{2,1,0:T(8,128)(2,1)} async-done(((bf16[8,16,5120]{2,1,0:T(8,128)(2,1)}), bf16[8,16,5120]{2,1,0:T(8,128)(2,1)}, u32[]{:S(2)}, u32[]{:S(2)}) %all-to-all-start) | async-done | bytes 1310752 | tf_op jit(solution)/shard_map/all_to_all | solution.py:142
  69.1 3.0 %fusion.2 = f32[352]{0:T(512)S(1)} fusion(bf16[128,5120]{1,0:T(8,128)(2,1)} %bitcast.2, bf16[224,5120]{1,0:T(8,128)(2,1)} %all-gather.2.cloned.1.call-done), kind=kLoop, calls=%fused_computation.6 | loop fusion | flops 10813088 | bytes 3605888 | tf_op jit(solution)/shard_map/reduce_sum | solution.py:18
  72.1 2.1 %fusion.4 = bf16[352,5120]{1,0:T(8,128)(2,1)S(1)} fusion(f32[5120]{0:T(1024)S(1)} %copy-done.5, f32[352]{0:T(512)S(1)} %add_rsqrt_fusion.2, bf16[128,5120]{1,0:T(8,128)(2,1)} %bitcast.2, bf16[224,5120]{1,0:T(8,128)(2,1)S(1)} %copy-done.1), kind=kLoop, calls=%fused_computation.8 | loop fusion | flops 12615680 | bytes 7230848 | tf_op jit(solution)/shard_map/convert_element_type | solution.py:65
  74.2 1.8 %copy-done.2 = bf16[352,5120]{1,0:T(8,128)(2,1)} copy-done((bf16[352,5120]{1,0:T(8,128)(2,1)}, bf16[352,5120]{1,0:T(8,128)(2,1)S(1)}, u32[]{:S(2)}) %copy-start.2) | copy-done | bytes 3604504
  76.0 1.1 %fusion.68 = f32[352,256]{1,0:T(8,128)S(1)} fusion(bf16[352,5120]{1,0:T(8,128)(2,1)S(1)} %fusion.4, bf16[5120,256]{1,0:T(8,128)(2,1)S(1)} %copy-done), kind=kOutput, calls=%fused_computation.131 | convolution fusion | flops 922746880 | bytes 6586368 | tf_op jit(solution)/shard_map/dot_general | solution.py:67
  77.4 0.4 multiply_reduce_fusion
  77.9 3.6 %multiply_reduce_fusion.1 = (f32[352]{0:T(512)S(1)}, f32[352,128]{1,0:T(8,128)S(1)}) fusion(bf16[352,5120]{1,0:T(8,128)(2,1)} %copy-done.2, bf16[5120,128]{1,0:T(8,128)(2,1)} %param.13), kind=kOutput, calls=%fused_computation.46 | convolution fusion | flops 461463200 | bytes 5096832 | tf_op jit(solution)/shard_map/dot_general | solution.py:73
  81.9 0.8 multiply_cosine_fusion
  83.0 0.3 fusion.13
  83.3 0.3 fusion.60
  83.6 1.2 %fusion.63 = (f32[2,224]{1,0:T(2,128)S(1)}, f32[2,224,224]{1,2,0:T(8,128)}) fusion(pred[224,224]{0,1:T(8,128)(4,1)S(1)} %copy-done.3, bf16[352,2,64]{2,0,1:T(8,128)(2,1)S(1)} %get-tuple-element.15, bf16[352,2,64]{2,0,1:T(8,128)(2,1)S(1)} %get-tuple-element.16, bf16[352,64]{1,0:T(8,128)(2,1)S(1)} %get-tuple-element.22, ...), kind=kOutput, calls=%fused_computation.130 | convolution fusion | flops 26435808 | bytes 723712 | tf_op jit(solution)/shard_map/sub | solution.py:86
  84.8 3.5 %convolution_convert_fusion.1 = bf16[352,128]{1,0:T(8,128)(2,1)S(1)} fusion(bf16[352,5120]{1,0:T(8,128)(2,1)} %copy-done.2, bf16[5120,128]{1,0:T(8,128)(2,1)} %param.14), kind=kOutput, calls=%fused_computation.23 | convolution fusion | flops 461418496 | bytes 5005312 | tf_op jit(solution)/shard_map/dot_general | solution.py:75
  88.4 0.3 fusion.14
  88.7 0.2 fusion.15
  89.0 2.2 %all_gather.7 = bf16[352,512]{1,0:T(8,128)(2,1)S(1)} all-gather(bf16[352,256]{1,0:T(8,128)(2,1)S(1)} %pad_maximum_fusion.1), channel_id=1, replica_groups=mesh['groups'=2,'dp'=8,'tensor'=2] {'tensor'}, dimensions={1}, use_global_device_ids=true | all-gather | bytes 540672 | tf_op jit(solution)/shard_map/all_gather | solution.py:161
  91.3 4.5 %convolution_add_fusion = bf16[352,2560]{1,0:T(8,128)(2,1)} fusion(bf16[352,512]{1,0:T(8,128)(2,1)S(1)} %all_gather.7, bf16[512,2560]{1,0:T(8,128)(2,1)} %bitcast.84, s32[]{:T(128)S(6)} %select_n.145, bf16[224,5120]{1,0:T(8,128)(2,1)} %all-gather.2.cloned.1.call-done, bf16[128,5120]{1,0:T(8,128)(2,1)} %bitcast.2), kind=kOutput, calls=%fused_computation.9 | convolution fusion | flops 928153600 | bytes 8388612 | tf_op jit(solution)/shard_map/dot_general | solution.py:163
  95.8 3.6 %gather_fusion.1 = bf16[160,2560]{1,0:T(8,128)(2,1)S(1)} fusion(bf16[352,2560]{1,0:T(8,128)(2,1)} %convolution_add_fusion, s32[1024]{0:T(1024)S(1)} %pad_clamp_fusion), kind=kCustom, calls=%fused_computation.1 | custom fusion | bytes 1639040 | tf_op jit(solution)/shard_map/jit(_take)/gather | solution.py:165
  99.5 1.3 %select_convert_fusion = bf16[160,2560]{1,0:T(8,128)(2,1)} fusion(bf16[160,2560]{1,0:T(8,128)(2,1)S(1)} %gather_fusion.1, pred[160]{0:T(512)(128)(4,1)S(1)} %get-tuple-element.13, pred[160]{0:T(512)(128)(4,1)S(1)} %fusion.58), kind=kLoop, calls=%fused_computation.14 | loop fusion | flops 819200 | bytes 1638720 | tf_op jit(solution)/shard_map/convert_element_type | solution.py:166
  (70 shorter events, 2.5 us)
Async XLA Ops:
  6.5 69.5 %copy-start = (bf16[5120,256]{1,0:T(8,128)(2,1)S(1)}, bf16[5120,256]{1,0:T(8,128)(2,1)}, u32[]{:S(2)}) copy-start(bf16[5120,256]{1,0:T(8,128)(2,1)} %param.12) | copy-start | bytes 7864324
  6.5 16.0 %all-gather.2.cloned.1.call-start = ((), (), s32[]{:S(2)}) async-start(), calls=%async_computation.2 | async-start | bytes 3440640 | tf_op jit(solution)/shard_map/all_gather | solution.py:60
  11.7 5.3 %copy-start.6 = (s32[8,5]{1,0:T(8,128)S(1)}, s32[8,5]{1,0:T(8,128)}, u32[]{:S(2)}) copy-start(s32[8,5]{1,0:T(8,128)} %param.19) | copy-start | bytes 484
  11.7 5.4 %copy-start.4 = (s32[8,5]{1,0:T(8,128)S(1)}, s32[8,5]{1,0:T(8,128)}, u32[]{:S(2)}) copy-start(s32[8,5]{1,0:T(8,128)} %param.18) | copy-start | bytes 484
  11.7 19.0 %all-to-all-start.1 = ((bf16[256,2,2560]{0,2,1:T(8,128)(2,1)}), bf16[256,2,2560]{0,2,1:T(8,128)(2,1)}, u32[]{:S(2)}, u32[]{:S(2)}) async-start(bf16[256,2,2560]{0,2,1:T(8,128)(2,1)} %bitcast.82), calls=%async_computation.1 | async-start | bytes 5242880 | tf_op jit(solution)/shard_map/all_to_all | solution.py:162
  30.7 38.3 %all-to-all-start = ((bf16[8,16,5120]{2,1,0:T(8,128)(2,1)}), bf16[8,16,5120]{2,1,0:T(8,128)(2,1)}, u32[]{:S(2)}, u32[]{:S(2)}) async-start(bf16[8,16,5120]{2,1,0:T(8,128)(2,1)} %broadcast_select_fusion), calls=%async_computation | async-start | bytes 2621440 | tf_op jit(solution)/shard_map/all_to_all | solution.py:142
  42.0 30.0 %copy-start.5 = (f32[5120]{0:T(1024)S(1)}, f32[5120]{0:T(1024)}, u32[]{:S(2)}) copy-start(f32[5120]{0:T(1024)} %param.11) | copy-start | bytes 61444
  69.1 3.0 %copy-start.1 = (bf16[224,5120]{1,0:T(8,128)(2,1)S(1)}, bf16[224,5120]{1,0:T(8,128)(2,1)}, u32[]{:S(2)}) copy-start(bf16[224,5120]{1,0:T(8,128)(2,1)} %all-gather.2.cloned.1.call-done) | copy-start | bytes 6881284
  74.2 1.8 %copy-start.2 = (bf16[352,5120]{1,0:T(8,128)(2,1)}, bf16[352,5120]{1,0:T(8,128)(2,1)S(1)}, u32[]{:S(2)}) copy-start(bf16[352,5120]{1,0:T(8,128)(2,1)S(1)} %fusion.4) | copy-start | bytes 10813444
  77.9 3.7 %copy-start.7 = (f32[128]{0:T(128)S(1)}, f32[128]{0:T(128)}, u32[]{:S(2)}) copy-start(f32[128]{0:T(128)} %param.16) | copy-start | bytes 1540
  77.9 3.8 %copy-start.8 = (f32[128]{0:T(128)S(1)}, f32[128]{0:T(128)}, u32[]{:S(2)}) copy-start(f32[128]{0:T(128)} %param.17) | copy-start | bytes 1540
  77.9 3.9 %copy-start.9 = (f32[64]{0:T(128)S(1)}, f32[64]{0:T(128)}, u32[]{:S(2)}) copy-start(f32[64]{0:T(128)} %multiply_power_fusion) | copy-start | bytes 772
  81.5 2.1 %copy-start.3 = (pred[224,224]{0,1:T(8,128)(4,1)S(1)}, pred[224,224]{0,1:T(8,128)(4,1)}, u32[]{:S(2)}) copy-start(pred[224,224]{0,1:T(8,128)(4,1)} %compare_and_fusion) | copy-start | bytes 150532
  84.8 3.6 %copy-start.10 = (f32[2,224,224]{1,2,0:T(8,128)S(1)}, f32[2,224,224]{1,2,0:T(8,128)}, u32[]{:S(2)}) copy-start(f32[2,224,224]{1,2,0:T(8,128)} %get-tuple-element.37) | copy-start | bytes 1204228
Sparse Core Ops, SparseCore 0:
  8.9 13.5 all-gather.1
where the time goes:
time: 108 us
  waiting for transfers between devices  30 us (28%)
  local copies, waits for them, and re-layouts  20.9 us (19%)
  matrix products  15.1 us (14%)
  other arithmetic  14.1 us (13%)
  between operations  13.8 us (13%)
  starting transfers between devices  11.6 us (11%)
  blocking collectives  2.24 us (2%)
    all_to_all x1, waiting for transfers between devices, per_device(): lax.all_to_all(outbound, 'dp', split_axis=0, concat_axis=0, tiled=True)  24.8 us
    all_to_all x1, starting transfers between devices, per_device(): lax.all_to_all(outbound, 'dp', split_axis=0, concat_axis=0, tiled=True)  6.46 us
    unnamed x24, local copies, waits for them, and re-layouts  6.35 us
    gather x1, local copies, waits for them, and re-layouts, per_device(): jnp.take(home_full, send_rows, axis=0).reshape(replicas, CAPP, -1)  5.64 us
    all_to_all x1, starting transfers between devices, per_device(): lax.all_to_all(o_weight, 'tensor', split_axis=1, concat_axis=0, tiled=True)  5.14 us
    dot_general x1, matrix products, per_device(): summed = jnp.dot(all_heads, own_columns, preferred_element_type=jnp.float32)  4.54 us
    all_gather x1, waiting for transfers between devices, widen(): return lax.all_gather(half_rows, 'tensor', axis=1, tiled=True)  4.41 us
    all_to_all x1, local copies, waits for them, and re-layouts, per_device(): lax.all_to_all(o_weight, 'tensor', split_axis=1, concat_axis=0, tiled=True)  4.4 us
  transfers between devices with their start and end apart: 3, of which 2 were waited for; matrix products, arithmetic and copies ran while one was open for 19% of the time, Pallas kernels for 0%

commit v1 on v0

v1 whole, which is shorter than its diff:
```python
import functools

import jax
import jax.numpy as jnp
import numpy as np
from jax import lax
from jax.experimental import pallas as pl
from jax.experimental.pallas import tpu as pltpu
from jax.sharding import PartitionSpec as P

HD = 128
CAPP = 16
LONG = 160
SHORT = 8
CHUNK = 512

EPSILON = 1e-06
ROPE_BASE = 1000000.0
MASKED_SCORE = -1e30
MESH = pl.DeviceIdType.MESH
F32 = jnp.float32
BF16 = jnp.bfloat16


def one_hot(hit):
    return jnp.where(hit, 1.0, 0.0).astype(BF16)


def dot(a, b):
    return jnp.dot(a, b, preferred_element_type=F32)


def head_norm(entries, gain):
    mean_square = jnp.mean(entries * entries, axis=-1, keepdims=True)
    return entries * lax.rsqrt(mean_square + EPSILON) * gain


def kernel(
    replicas,
    lens_ref,
    dest_ref,
    rope_ref,
    q_gain_ref,
    k_gain_ref,
    gain_ref,
    x_hbm,
    qw_hbm,
    kw_hbm,
    vw_hbm,
    o_hbm,
    out_hbm,
    x_own,
    x_other,
    w_all,
    o_all,
    x_send,
    x_recv,
    h_own,
    h_other,
    h_send,
    h_recv,
    qkv,
    out_buf,
    load_sem,
    pair_send,
    pair_recv,
    xs_sem,
    xr_sem,
    hs_sem,
    hr_sem,
    out_sem,
):
    me = lax.axis_index("dp")
    part = lax.axis_index("tensor")
    home, half = x_own.shape
    work = out_buf.shape[0]
    slots = lens_ref.shape[1]
    chunks = half // CHUNK
    peers = [lax.rem(me + k, replicas) for k in range(replicas)]

    barrier = pltpu.get_barrier_semaphore()
    for k in range(1, replicas):
        pl.semaphore_signal(barrier, inc=1, device_id={"dp": peers[k]}, device_id_type=MESH)
    pl.semaphore_signal(barrier, inc=1, device_id={"tensor": 1 - part}, device_id_type=MESH)

    own_cols = pl.ds(pl.multiple_of(part * half, CHUNK), half)
    other_cols = pl.ds(pl.multiple_of((1 - part) * half, CHUNK), half)
    loads = [
        pltpu.make_async_copy(x_hbm, x_own, load_sem.at[0]),
        pltpu.make_async_copy(qw_hbm, w_all.at[:, pl.ds(0, 2 * HD)], load_sem.at[1]),
        pltpu.make_async_copy(kw_hbm, w_all.at[:, pl.ds(2 * HD, HD)], load_sem.at[2]),
        pltpu.make_async_copy(vw_hbm, w_all.at[:, pl.ds(3 * HD, HD)], load_sem.at[3]),
        pltpu.make_async_copy(o_hbm.at[:, own_cols], o_all.at[0], load_sem.at[4]),
    ]
    for load in loads:
        load.start()

    lens = [lens_ref[me, s] for s in range(slots)]
    dests = [dest_ref[me, s] for s in range(slots)]
    row = lax.broadcasted_iota(jnp.int32, (1, home), 1)
    col = lax.broadcasted_iota(jnp.int32, (home, 1), 0)
    to_send = jnp.full((1, home), -1, jnp.int32)
    to_work = jnp.full((1, home), -1, jnp.int32)
    start = jnp.zeros((home, 1), jnp.int32)
    offset = jnp.int32(0)
    staying = jnp.int32(0)
    for s in range(slots):
        before = jnp.int32(0)
        for t in range(s):
            before = before + jnp.where(dests[t] == dests[s], lens[t], 0)
        shift = dests[s] - me
        shift = jnp.where(shift < 0, shift + replicas, shift)
        stays = shift == 0
        send_base = jnp.where(stays, -home, shift * CAPP + before - offset)
        work_base = jnp.where(stays, before - offset, -2 * home)
        to_send = jnp.where(row >= offset, row + send_base - jnp.where(stays, home, 0), to_send)
        to_work = jnp.where(row >= offset, row + work_base, to_work)
        start = jnp.where(col >= offset, offset, start)
        staying = staying + jnp.where(stays, lens[s], 0)
        offset = offset + lens[s]
    to_send = jnp.where(row >= offset, -1, to_send)
    to_work = jnp.where(row >= offset, -1, to_work)
    pool = replicas * CAPP
    send_hot = one_hot(lax.broadcasted_iota(jnp.int32, (pool, home), 0) == to_send)

    x_recv[pl.ds(0, CAPP), :] = jnp.zeros((CAPP, half), BF16)
    h_recv[pl.ds(0, CAPP), :] = jnp.zeros((CAPP, h_recv.shape[1]), BF16)

    loads[0].wait()

    @pl.loop(0, chunks)
    def _(c):
        cols = pl.ds(pl.multiple_of(c * CHUNK, CHUNK), CHUNK)
        x_send[:, cols] = dot(send_hot, x_own[:, cols]).astype(BF16)

    pl.semaphore_wait(barrier, replicas)

    pair_x = pltpu.make_async_remote_copy(
        x_own, x_other, pair_send.at[0], pair_recv.at[0], {"tensor": 1 - part}, MESH
    )
    pair_x.start()

    def exchange(source, target, send_sem, recv_sem):
        copies = []
        for k in range(1, replicas):
            copies.append(
                pltpu.make_async_remote_copy(
                    source.at[pl.ds(k * CAPP, CAPP)],
                    target.at[pl.ds((replicas - k) * CAPP, CAPP)],
                    send_sem.at[k],
                    recv_sem.at[replicas - k],
                    {"dp": peers[k]},
                    MESH,
                )
            )
        for copy in copies:
            copy.start()
        return copies

    x_copies = exchange(x_send, x_recv, xs_sem, xr_sem)
    pair_o = pltpu.make_async_remote_copy(
        o_hbm.at[:, other_cols], o_all.at[1], pair_send.at[1], pair_recv.at[1], {"tensor": 1 - part}, MESH
    )
    pair_o.start()

    slot = lax.broadcasted_iota(jnp.int32, (1, pool), 1)
    from_pool = jnp.full((1, pool), -1, jnp.int32)
    begin = staying
    for k in range(1, replicas):
        count = jnp.int32(0)
        for s in range(slots):
            count = count + jnp.where(dest_ref[peers[k], s] == me, lens_ref[peers[k], s], 0)
        inside = (slot >= k * CAPP) & (slot < k * CAPP + count)
        from_pool = jnp.where(inside, slot + (begin - k * CAPP), from_pool)
        begin = begin + count
    home_hot = one_hot(lax.broadcasted_iota(jnp.int32, (work, home), 0) == to_work)
    pool_hot = one_hot(lax.broadcasted_iota(jnp.int32, (work, pool), 0) == from_pool)

    angles = (col - start).astype(F32) * rope_ref[0:1, :]
    cosine = jnp.cos(angles)
    sine = jnp.sin(angles) * rope_ref[1:2, :]

    def square_sum(x_ref):
        def step(c, total):
            for piece in range(CHUNK // 128):
                cols = pl.ds(pl.multiple_of(c * CHUNK + piece * 128, 128), 128)
                wide = x_ref[:, cols].astype(F32)
                total = total + wide * wide
            return total

        return lax.fori_loop(0, chunks, step, jnp.zeros((home, 128), F32))

    own_squares = square_sum(x_own)
    pair_x.wait_recv()
    squares = own_squares + square_sum(x_other)
    scale = lax.rsqrt(jnp.sum(squares, axis=1, keepdims=True) / (2 * half) + EPSILON)
    for load in loads[1:4]:
        load.wait()
    qkv[...] = jnp.zeros_like(qkv)
    for x_ref, base in ((x_own, part * half), (x_other, (1 - part) * half)):

        @pl.loop(0, chunks)
        def _(c, x_ref=x_ref, base=base):
            cols = pl.ds(pl.multiple_of(c * CHUNK, CHUNK), CHUNK)
            rows = pl.ds(pl.multiple_of(base + c * CHUNK, CHUNK), CHUNK)
            normed = (x_ref[:, cols].astype(F32) * scale * gain_ref[:, rows]).astype(BF16)
            qkv[...] += dot(normed, w_all[rows, :])

    def rotated(entries, gain):
        entries = head_norm(entries, gain)
        return (entries * cosine + pltpu.roll(entries, HD // 2, 1) * sine).astype(BF16)

    keys = rotated(qkv[:, pl.ds(2 * HD, HD)], k_gain_ref[...])
    values = qkv[:, pl.ds(3 * HD, HD)].astype(BF16)
    key_id = lax.broadcasted_iota(jnp.int32, (home, home), 1)
    query_id = lax.broadcasted_iota(jnp.int32, (home, home), 0)
    allowed = (key_id >= start) & (key_id <= query_id)
    for h in range(2):
        queries = rotated(qkv[:, pl.ds(h * HD, HD)], q_gain_ref[...])
        scores = lax.dot_general(
            queries, keys, (((1,), (1,)), ((), ())), preferred_element_type=F32
        ) * HD ** (-0.5)
        scores = jnp.where(allowed, scores, MASKED_SCORE)
        exp_scores = jnp.exp(scores - jnp.max(scores, axis=1, keepdims=True))
        weights = (exp_scores / jnp.sum(exp_scores, axis=1, keepdims=True)).astype(BF16)
        h_own[:, pl.ds(h * HD, HD)] = dot(weights, values).astype(BF16)

    pair_h = pltpu.make_async_remote_copy(
        h_own, h_other, pair_send.at[2], pair_recv.at[2], {"tensor": 1 - part}, MESH
    )
    pair_h.start()
    width = h_own.shape[1]
    h_send[:, pl.ds(0, width)] = dot(send_hot, h_own[...]).astype(BF16)
    pair_h.wait_recv()
    h_send[:, pl.ds(width, width)] = dot(send_hot, h_other[...]).astype(BF16)
    h_copies = exchange(h_send, h_recv, hs_sem, hr_sem)

    home_own = dot(home_hot, h_own[...])
    home_other = dot(home_hot, h_other[...])
    for copy in x_copies:
        copy.wait_recv()
    for copy in h_copies:
        copy.wait_recv()
    loads[4].wait()
    pair_o.wait_recv()
    all_own = (home_own + dot(pool_hot, h_recv[:, pl.ds(0, width)])).astype(BF16)
    all_other = (home_other + dot(pool_hot, h_recv[:, pl.ds(width, width)])).astype(BF16)

    @pl.loop(0, chunks)
    def _(c):
        cols = pl.ds(pl.multiple_of(c * CHUNK, CHUNK), CHUNK)
        moved = dot(home_hot, x_own[:, cols]) + dot(pool_hot, x_recv[:, cols])
        attended = dot(all_own, o_all[0, :, cols]) + dot(all_other, o_all[1, :, cols])
        out_buf[:, cols] = (moved + attended).astype(BF16)

    result = pltpu.make_async_copy(out_buf, out_hbm, out_sem)
    result.start()
    for copy in [pair_x, pair_o, pair_h] + x_copies + h_copies:
        copy.wait_send()
    result.wait()


def per_device(
    hidden_states,
    input_gain,
    q_weight,
    k_weight,
    v_weight,
    o_weight,
    q_gain,
    k_gain,
    seq_lens,
    dest,
):
    replicas = lax.axis_size("dp")
    home, half = hidden_states.shape
    slots = seq_lens.shape[1]
    work = max(LONG, slots * SHORT + (slots - 1) * CAPP)
    pool = replicas * CAPP
    width = o_weight.shape[0]
    channel = np.arange(HD)
    frequency = ROPE_BASE ** (-2.0 * (channel % (HD // 2)) / HD)
    sign = np.where(channel < HD // 2, -1.0, 1.0)
    rope = jnp.asarray(np.stack([frequency, sign]).astype(np.float32))
    vmem = pl.BlockSpec(memory_space=pltpu.VMEM)
    smem = pl.BlockSpec(memory_space=pltpu.SMEM)
    hbm = pl.BlockSpec(memory_space=pl.ANY)
    dma = pltpu.SemaphoreType.DMA
    return pl.pallas_call(
        functools.partial(kernel, replicas),
        out_shape=jax.ShapeDtypeStruct((work, half), BF16),
        in_specs=[smem, smem, vmem, vmem, vmem, vmem] + [hbm] * 5,
        out_specs=hbm,
        scratch_shapes=[
            pltpu.VMEM((home, half), BF16),
            pltpu.VMEM((home, half), BF16),
            pltpu.VMEM((2 * half, 4 * HD), BF16),
            pltpu.VMEM((2, width, half), BF16),
            pltpu.VMEM((pool, half), BF16),
            pltpu.VMEM((pool, half), BF16),
            pltpu.VMEM((home, width), BF16),
            pltpu.VMEM((home, width), BF16),
            pltpu.VMEM((pool, 2 * width), BF16),
            pltpu.VMEM((pool, 2 * width), BF16),
            pltpu.VMEM((home, 4 * HD), F32),
            pltpu.VMEM((work, half), BF16),
            dma((5,)),
            dma((3,)),
            dma((3,)),
            dma((replicas,)),
            dma((replicas,)),
            dma((replicas,)),
            dma((replicas,)),
            dma,
        ],
        compiler_params=pltpu.CompilerParams(
            collective_id=0,
            has_side_effects=True,
            vmem_limit_bytes=56 * 1024 * 1024,
        ),
    )(
        seq_lens,
        dest,
        rope,
        q_gain.reshape(1, HD),
        k_gain.reshape(1, HD),
        input_gain.reshape(1, -1),
        hidden_states,
        q_weight,
        k_weight,
        v_weight,
        o_weight,
    )


def solution(mesh):
    return jax.shard_map(
        per_device,
        mesh=mesh,
        in_specs=(
            P(("groups", "dp"), "tensor"),
            P(),
            P(None, "tensor"),
            P(None, "tensor"),
            P(None, "tensor"),
            P("tensor", None),
            P(),
            P(),
            P("groups", None),
            P("groups", None),
        ),
        out_specs=P(("groups", "dp"), "tensor"),
        check_vma=False,
    )
```

time: 108 us -> 30.7 us (0.28)
  waiting for transfers between devices: 30 us -> 0 us
  Pallas kernels: 0 us -> 28.4 us
  local copies, waits for them, and re-layouts: 20.9 us -> 2.09 us
  matrix products: 15.1 us -> 0 us
  other arithmetic: 14.1 us -> 0 us
  between operations: 13.8 us -> 0.01 us
  starting transfers between devices: 11.6 us -> 0 us
  blocking collectives: 2.24 us -> 0 us
    pallas_call x0 -> x1, Pallas kernels: none -> 28.4 us  [per_device(): pl.pallas_call(functools.partial(kernel, replicas), out_shape=jax.ShapeDt...]
    all_to_all x2 -> x0, waiting for transfers between devices: 24.8 us -> none  [the longest x1 24.8 us: per_device(): lax.all_to_all(outbound, 'dp', split_axis=0, concat_axis=0, tiled=True)]
    dot_general x7 -> x0, matrix products: 13.6 us -> none  [the longest x1 4.54 us: per_device(): summed = jnp.dot(all_heads, own_columns, preferred_element_type=jnp.float32)]
    all_to_all x2 -> x0, starting transfers between devices: 11.6 us -> none  [the longest x1 6.46 us: per_device(): lax.all_to_all(outbound, 'dp', split_axis=0, concat_axis=0, tiled=True)]
    gather x2 -> x0, local copies, waits for them, and re-layouts: 9.26 us -> none  [the longest x1 5.64 us: per_device(): jnp.take(home_full, send_rows, axis=0).reshape(replicas, CAPP, -1)]
    all_gather x1 -> x0, waiting for transfers between devices: 4.41 us -> none  [widen(): return lax.all_gather(half_rows, 'tensor', axis=1, tiled=True)]
    all_to_all x1 -> x0, local copies, waits for them, and re-layouts: 4.4 us -> none  [per_device(): lax.all_to_all(o_weight, 'tensor', split_axis=1, concat_axis=0, tiled=True)]
    reduce_sum x7 -> x0, other arithmetic: 4.4 us -> none  [the longest x2 3.43 us: rms_scale(): mean_square = jnp.mean(entries * entries, axis=-1, keepdims=True)]
  transfers between devices with their start and end apart: 3 -> 0, of which waited for: 2 -> 0; matrix products, arithmetic and copies ran while one was open for 19% -> 0% of each run, Pallas kernels for 0% -> 0%
where the time goes in v1:
time: 30.7 us; the launch traced here: 30.5 us
  Pallas kernels  28.4 us (93%)
  local copies, waits for them, and re-layouts  2.09 us (7%)
    pallas_call x1, Pallas kernels, per_device(): pl.pallas_call(functools.partial(kernel, replicas), out_shape=jax.ShapeDt...  28.4 us
    unnamed x1, local copies, waits for them, and re-layouts  2.09 us

profile of v1, /device:TPU:0, one launch (start us, length us, event | category | flops | bytes accessed | tf_op | source)
XLA Modules:
  0.0 30.5 jit_solution(15549456900349077601)
XLA Ops:
  0.0 28.4 %shard_map.109 = bf16[160,2560]{1,0:T(8,128)(2,1)} custom-call(s32[8,5]{1,0:T(8,128)} %lens_ref.1, s32[8,5]{1,0:T(8,128)} %dest_ref.1, f32[2,128]{1,0:T(2,128)} %constant.2.clone.rope_ref, f32[1,128]{1,0:T(1,128)} %bitcast.4, f32[1,128]{1,0:T(1,128)} %bitcast.5, f32[1,5120]{1,0:T(1,128)} %bitcast.3, bf16[224,2560]{1,0:T(8,128)(2,1)} %x_hbm.1, ...), custom_call_target="tpu_custom_call" | custom-call | tf_op jit(solution)/shard_map/pallas_call | solution.py:289
  28.4 2.1 %copy.13 = bf16[160,2560]{1,0:T(8,128)(2,1)} copy(bf16[160,2560]{1,0:T(8,128)(2,1)} %shard_map.109) | data formatting | bytes 1638400

commit v2 on v1

--- a/solution.py
+++ b/solution.py
@@ -13,6 +13,7 @@
 LONG = 160
 SHORT = 8
 CHUNK = 512
+WIDE = 1280
 
 EPSILON = 1e-06
 ROPE_BASE = 1000000.0
@@ -59,7 +60,11 @@
     h_other,
     h_send,
     h_recv,
+    h_pass,
+    squares_own,
+    squares_other,
     qkv,
+    result,
     out_buf,
     load_sem,
     pair_send,
@@ -76,6 +81,9 @@
     work = out_buf.shape[0]
     slots = lens_ref.shape[1]
     chunks = half // CHUNK
+    ahead = chunks * 2 // 5
+    early = pl.ds(0, ahead * CHUNK)
+    late = pl.ds(ahead * CHUNK, half - ahead * CHUNK)
     peers = [lax.rem(me + k, replicas) for k in range(replicas)]
 
     barrier = pltpu.get_barrier_semaphore()
@@ -133,7 +141,18 @@
         cols = pl.ds(pl.multiple_of(c * CHUNK, CHUNK), CHUNK)
         x_send[:, cols] = dot(send_hot, x_own[:, cols]).astype(BF16)
 
+    def square_sum(x_ref):
+        def step(c, total):
+            for piece in range(CHUNK // 128):
+                cols = pl.ds(pl.multiple_of(c * CHUNK + piece * 128, 128), 128)
+                wide = x_ref[:, cols].astype(F32)
+                total = total + wide * wide
+            return total
+
+        return lax.fori_loop(0, chunks, step, jnp.zeros((home, 128), F32))
+
     pl.semaphore_wait(barrier, replicas)
+
 
     pair_x = pltpu.make_async_remote_copy(
         x_own, x_other, pair_send.at[0], pair_recv.at[0], {"tensor": 1 - part}, MESH
@@ -157,11 +176,15 @@
             copy.start()
         return copies
 
-    x_copies = exchange(x_send, x_recv, xs_sem, xr_sem)
+    x_first = exchange(x_send.at[:, early], x_recv.at[:, early], xs_sem.at[0], xr_sem.at[0])
+    squares_own[...] = square_sum(x_own)
+    pair_s = pltpu.make_async_remote_copy(
+        squares_own, squares_other, pair_send.at[3], pair_recv.at[3], {"tensor": 1 - part}, MESH
+    )
+    pair_s.start()
     pair_o = pltpu.make_async_remote_copy(
         o_hbm.at[:, other_cols], o_all.at[1], pair_send.at[1], pair_recv.at[1], {"tensor": 1 - part}, MESH
     )
-    pair_o.start()
 
     slot = lax.broadcasted_iota(jnp.int32, (1, pool), 1)
     from_pool = jnp.full((1, pool), -1, jnp.int32)
@@ -180,31 +203,25 @@
     cosine = jnp.cos(angles)
     sine = jnp.sin(angles) * rope_ref[1:2, :]
 
-    def square_sum(x_ref):
-        def step(c, total):
-            for piece in range(CHUNK // 128):
-                cols = pl.ds(pl.multiple_of(c * CHUNK + piece * 128, 128), 128)
-                wide = x_ref[:, cols].astype(F32)
-                total = total + wide * wide
-            return total
-
-        return lax.fori_loop(0, chunks, step, jnp.zeros((home, 128), F32))
-
-    own_squares = square_sum(x_own)
-    pair_x.wait_recv()
-    squares = own_squares + square_sum(x_other)
-    scale = lax.rsqrt(jnp.sum(squares, axis=1, keepdims=True) / (2 * half) + EPSILON)
     for load in loads[1:4]:
         load.wait()
-    qkv[...] = jnp.zeros_like(qkv)
-    for x_ref, base in ((x_own, part * half), (x_other, (1 - part) * half)):
-
-        @pl.loop(0, chunks)
-        def _(c, x_ref=x_ref, base=base):
-            cols = pl.ds(pl.multiple_of(c * CHUNK, CHUNK), CHUNK)
-            rows = pl.ds(pl.multiple_of(base + c * CHUNK, CHUNK), CHUNK)
-            normed = (x_ref[:, cols].astype(F32) * scale * gain_ref[:, rows]).astype(BF16)
-            qkv[...] += dot(normed, w_all[rows, :])
+    pair_s.wait_recv()
+    squares = squares_own[...] + squares_other[...]
+    scale = lax.rsqrt(jnp.sum(squares, axis=1, keepdims=True) / (2 * half) + EPSILON)
+
+    def project(x_ref, base, step):
+        cols = pl.ds(step * WIDE, WIDE)
+        rows = pl.ds(pl.multiple_of(base + step * WIDE, WIDE), WIDE)
+        normed = (x_ref[:, cols].astype(F32) * scale * gain_ref[:, rows]).astype(BF16)
+        return dot(normed, w_all[rows, :])
+
+    qkv[...] = project(x_own, part * half, 0)
+    for step in range(1, half // WIDE):
+        qkv[...] += project(x_own, part * half, step)
+    pair_x.wait_recv()
+    pair_o.start()
+    for step in range(half // WIDE):
+        qkv[...] += project(x_other, (1 - part) * half, step)
 
     def rotated(entries, gain):
         entries = head_norm(entries, gain)
@@ -225,39 +242,60 @@
         weights = (exp_scores / jnp.sum(exp_scores, axis=1, keepdims=True)).astype(BF16)
         h_own[:, pl.ds(h * HD, HD)] = dot(weights, values).astype(BF16)
 
+    h_send[...] = dot(send_hot, h_own[...]).astype(BF16)
+    h_copies = exchange(h_send, h_recv, hs_sem, hr_sem)
+    x_last = exchange(x_send.at[:, late], x_recv.at[:, late], xs_sem.at[1], xr_sem.at[1])
     pair_h = pltpu.make_async_remote_copy(
         h_own, h_other, pair_send.at[2], pair_recv.at[2], {"tensor": 1 - part}, MESH
     )
     pair_h.start()
-    width = h_own.shape[1]
-    h_send[:, pl.ds(0, width)] = dot(send_hot, h_own[...]).astype(BF16)
+    loads[4].wait()
+    home_own = dot(home_hot, h_own[...]).astype(BF16)
     pair_h.wait_recv()
-    h_send[:, pl.ds(width, width)] = dot(send_hot, h_other[...]).astype(BF16)
-    h_copies = exchange(h_send, h_recv, hs_sem, hr_sem)
-
-    home_own = dot(home_hot, h_own[...])
-    home_other = dot(home_hot, h_other[...])
-    for copy in x_copies:
-        copy.wait_recv()
-    for copy in h_copies:
-        copy.wait_recv()
-    loads[4].wait()
+    home_other = dot(home_hot, h_other[...]).astype(BF16)
     pair_o.wait_recv()
-    all_own = (home_own + dot(pool_hot, h_recv[:, pl.ds(0, width)])).astype(BF16)
-    all_other = (home_other + dot(pool_hot, h_recv[:, pl.ds(width, width)])).astype(BF16)
 
     @pl.loop(0, chunks)
     def _(c):
         cols = pl.ds(pl.multiple_of(c * CHUNK, CHUNK), CHUNK)
-        moved = dot(home_hot, x_own[:, cols]) + dot(pool_hot, x_recv[:, cols])
-        attended = dot(all_own, o_all[0, :, cols]) + dot(all_other, o_all[1, :, cols])
-        out_buf[:, cols] = (moved + attended).astype(BF16)
-
-    result = pltpu.make_async_copy(out_buf, out_hbm, out_sem)
-    result.start()
-    for copy in [pair_x, pair_o, pair_h] + x_copies + h_copies:
+        attended = dot(home_own, o_all[0, :, cols]) + dot(home_other, o_all[1, :, cols])
+        result[:, cols] = dot(home_hot, x_own[:, cols]) + attended
+
+    for copy in h_copies:
+        copy.wait_recv()
+    pair_r = pltpu.make_async_remote_copy(
+        h_recv, h_pass, pair_send.at[4], pair_recv.at[4], {"tensor": 1 - part}, MESH
+    )
+    pair_r.start()
+    pool_own = dot(pool_hot, h_recv[...]).astype(BF16)
+
+    @pl.loop(0, chunks)
+    def _(c):
+        cols = pl.ds(pl.multiple_of(c * CHUNK, CHUNK), CHUNK)
+        result[:, cols] += dot(pool_own, o_all[0, :, cols])
+
+    pair_r.wait_recv()
+    pool_other = dot(pool_hot, h_pass[...]).astype(BF16)
+
+    @pl.loop(0, chunks)
+    def _(c):
+        cols = pl.ds(pl.multiple_of(c * CHUNK, CHUNK), CHUNK)
+        result[:, cols] += dot(pool_other, o_all[1, :, cols])
+
+    writes = []
+    for c in range(chunks):
+        if c in (0, ahead):
+            for copy in x_first if c == 0 else x_last:
+                copy.wait_recv()
+        cols = pl.ds(c * CHUNK, CHUNK)
+        out_buf[:, cols] = (result[:, cols] + dot(pool_hot, x_recv[:, cols])).astype(BF16)
+        write = pltpu.make_async_copy(out_buf.at[:, cols], out_hbm.at[:, cols], out_sem.at[c])
+        write.start()
+        writes.append(write)
+    for copy in [pair_s, pair_x, pair_o, pair_h, pair_r] + x_first + x_last + h_copies:
         copy.wait_send()
-    result.wait()
+    for write in writes:
+        write.wait()
 
 
 def per_device(
@@ -300,18 +338,22 @@
             pltpu.VMEM((pool, half), BF16),
             pltpu.VMEM((home, width), BF16),
             pltpu.VMEM((home, width), BF16),
-            pltpu.VMEM((pool, 2 * width), BF16),
-            pltpu.VMEM((pool, 2 * width), BF16),
+            pltpu.VMEM((pool, width), BF16),
+            pltpu.VMEM((pool, width), BF16),
+            pltpu.VMEM((pool, width), BF16),
+            pltpu.VMEM((home, 128), F32),
+            pltpu.VMEM((home, 128), F32),
             pltpu.VMEM((home, 4 * HD), F32),
+            pltpu.VMEM((work, half), F32),
             pltpu.VMEM((work, half), BF16),
             dma((5,)),
-            dma((3,)),
-            dma((3,)),
+            dma((5,)),
+            dma((5,)),
+            dma((2, replicas)),
+            dma((2, replicas)),
             dma((replicas,)),
             dma((replicas,)),
-            dma((replicas,)),
-            dma((replicas,)),
-            dma,
+            dma((half // CHUNK,)),
         ],
         compiler_params=pltpu.CompilerParams(
             collective_id=0,

time: 30.7 us -> 25.1 us (0.82)
  Pallas kernels: 28.4 us -> 22.8 us
    pallas_call x1, Pallas kernels: 28.4 us -> 22.8 us  [per_device(): pl.pallas_call(functools.partial(kernel, replicas), out_shape=jax.ShapeDt...]
where the time goes in v2:
time: 25.1 us; the launch traced here: 24.9 us
  Pallas kernels  22.8 us (91%)
  local copies, waits for them, and re-layouts  2.09 us (8%)
    pallas_call x1, Pallas kernels, per_device(): pl.pallas_call(functools.partial(kernel, replicas), out_shape=jax.ShapeDt...  22.8 us
    unnamed x1, local copies, waits for them, and re-layouts  2.09 us

profile of v2, /device:TPU:0, one launch (start us, length us, event | category | flops | bytes accessed | tf_op | source)
XLA Modules:
  0.0 24.9 jit_solution(11438016594153885520)
XLA Ops:
  0.0 22.8 %shard_map.109 = bf16[160,2560]{1,0:T(8,128)(2,1)} custom-call(s32[8,5]{1,0:T(8,128)} %lens_ref.1, s32[8,5]{1,0:T(8,128)} %dest_ref.1, f32[2,128]{1,0:T(2,128)} %constant.2.clone.rope_ref, f32[1,128]{1,0:T(1,128)} %bitcast.4, f32[1,128]{1,0:T(1,128)} %bitcast.5, f32[1,5120]{1,0:T(1,128)} %bitcast.3, bf16[224,2560]{1,0:T(8,128)(2,1)} %x_hbm.1, ...), custom_call_target="tpu_custom_call" | custom-call | tf_op jit(solution)/shard_map/pallas_call | solution.py:327
  22.8 2.1 %copy.13 = bf16[160,2560]{1,0:T(8,128)(2,1)} copy(bf16[160,2560]{1,0:T(8,128)(2,1)} %shard_map.109) | data formatting | bytes 1638400
